TPU v7x, 128 devices: a whole 4x4x4 slice. The times are simulated.
128 devices in a mesh: rows: 32 (over z, y, core), cols: 4 (over x).
Axes of the slice: x: 4, y: 4, z: 4, core: 2. Of those that a mesh axis runs over, the one named last changes fastest.
Arguments:
- basis: float32 [64, 262144], P('cols', 'rows'), may hold values from -450 to 450
- blocks: bfloat16 [1024, 4, 256, 256], P('rows'), may hold values from -16 to 1, as said below
- far_cols: int32 [1024], P('rows'), may hold values from 0 to 1023, as said below
Outputs:
- basis_out: float32 [64, 262144], P('cols', 'rows')
- ritz: float32 [64, 64], P(None, 'cols')
Inputs may be any that keep to these rules, and one draw needn't show every extreme that they name: Off-diagonal entries are positive; each diagonal entry of a diagonal block is minus the sum of the other entries of its row over the four blocks, rounded to bfloat16. `far_cols`: the block rows of one device name at most 2 far columns among the block rows of any one device; the block rows of some device are named by exactly 2 block rows of every device.
All inputs are finite; a program needn't handle non-finite values.
Results may differ from a plain program's by a relative error of at most 0.0036.
Values may be sent and summed in bfloat16 or wider, within the bound.
No kernel may reach another device: no remote copies, remote signals or barrier semaphores. Data moves between devices by JAX's collectives and lax.ppermute only.
A program may use at most 128 MiB of HBM per device.

v0:
```python
import jax
import jax.numpy as jnp
from jax import lax
from jax.sharding import PartitionSpec as P

ITERS = 4


def with_halo(block, sides, width):
    for axis, dim in sides:
        count = lax.axis_size(axis)
        forward = [(i, i + 1) for i in range(count - 1)]
        forward.append((count - 1, 0))
        backward = [(target, source) for source, target in forward]
        low = lax.ppermute(
            lax.slice_in_dim(block, block.shape[dim] - width, None, axis=dim), axis, forward
        )
        high = lax.ppermute(lax.slice_in_dim(block, 0, width, axis=dim), axis, backward)
        block = jnp.concatenate([low, block, high], axis=dim)
    return block


def block_product(pieces, blocks, position):
    return jnp.einsum(
        "jbt,bst->jbs", pieces, blocks[:, position], preferred_element_type=jnp.float32
    )


def body(basis, blocks, far_cols):
    width = basis.shape[0]
    block_rows = blocks.shape[0]
    block_size = blocks.shape[2]
    row_devices = lax.axis_size("rows")
    total_states = block_rows * block_size * row_devices
    modes = width * lax.axis_size("cols")
    highest = lax.Precision.HIGHEST

    def apply_generator(iterate_bf):
        shaped = iterate_bf.reshape(width, block_rows, block_size)
        result = block_product(shaped, blocks, 0)
        empty = jnp.zeros((width, block_rows, block_size), jnp.bfloat16)
        piece = lax.all_gather(shaped, "rows", axis=1, tiled=True)
        inside = jnp.logical_and(far_cols >= 0, far_cols < piece.shape[1])
        taken = jnp.take(piece, jnp.clip(far_cols, 0, piece.shape[1] - 1), axis=1)
        remote = jnp.where(inside[None, :, None], taken, empty)
        extended = with_halo(shaped, (("rows", 1),), 1)
        result = result + block_product(extended[:, :-2], blocks, 1)
        result = result + block_product(extended[:, 2:], blocks, 2)
        result = result + block_product(remote, blocks, 3)
        return result.reshape(width, block_rows * block_size)

    iterate = basis
    for step in range(ITERS):
        iterate = iterate + 0.2 * apply_generator(iterate.astype(jnp.bfloat16))
    whole_iterate = lax.all_gather(iterate, "cols", axis=0, tiled=True)
    contract = (((1,), (1,)), ((), ()))
    gram_part = lax.dot_general(whole_iterate, iterate, contract, precision=highest)
    column_start = lax.axis_index("cols") * width
    gram_mine = lax.psum(gram_part, "rows")
    gram = lax.all_gather(gram_mine, "cols", axis=1, tiled=True) / total_states
    applied = apply_generator(iterate.astype(jnp.bfloat16))
    product_part = lax.dot_general(whole_iterate, applied, contract, precision=highest)
    product_mine = lax.psum(product_part, "rows")
    product = lax.all_gather(product_mine, "cols", axis=1, tiled=True) / total_states
    factor = jnp.linalg.cholesky(gram)
    identity_square = jnp.eye(modes, dtype=factor.dtype)
    inverse_factor = lax.linalg.triangular_solve(
        factor, identity_square, left_side=True, lower=True
    )
    own_rows = lax.dynamic_slice_in_dim(inverse_factor, column_start, width, 0)
    basis_out = jnp.dot(own_rows, whole_iterate, precision=highest)
    left_part = jnp.dot(inverse_factor, product, precision=highest)
    ritz_whole = jnp.dot(left_part, inverse_factor.T, precision=highest)
    ritz = lax.dynamic_slice_in_dim(ritz_whole, column_start, width, 1)
    return (basis_out, ritz)


def solution(mesh):
    in_specs = (P("cols", "rows"), P("rows", None, None, None), P("rows"))
    out_specs = (P("cols", "rows"), P(None, "cols"))
    return jax.shard_map(body, mesh=mesh, in_specs=in_specs, out_specs=out_specs, check_vma=False)
```

profile of v0, /device:TPU:0, one launch (start us, length us, event | category | flops | bytes accessed | tf_op | source)
XLA Modules:
  0.0 539.1 jit_solution(13265493274930220181)
XLA Ops:
  7.2 1.1 convert_element_type.16
  8.3 0.7 copy.158
  9.1 0.7 fusion.238
  9.8 6.0 %collective-permute-start.1 = (bf16[16,1,256]{2,0,1:T(8,128)(2,1)S(1)}, bf16[16,1,256]{2,0,1:T(8,128)(2,1)S(1)}, u32[]{:S(2)}, u32[]{:S(2)}) collective-permute-start(bf16[16,1,256]{2,0,1:T(8,128)(2,1)S(1)} %get-tuple-element.23), channel_id=1, source_target_pairs={{4,0},{8,4},{12,8},{16,12},{20,16},{24,20},{28,24},{32,28},{36,32}... | collective-permute-start | bytes 24584 | tf_op jit(solution)/shard_map/ppermute | solution.py:18
  15.8 0.7 compare_and_fusion
  16.5 3.4 fusion.60
  19.9 3.6 fusion.84
  23.5 3.5 fusion.81
  27.0 39.3 %all-gather.7.cloned.1.call-done = bf16[16,1024,256]{2,0,1:T(8,128)(2,1)} async-done(((bf16[16,32,256]{2,0,1:T(8,128)(2,1)}), bf16[16,1024,256]{2,0,1:T(8,128)(2,1)}) %all-gather.7.cloned.1.call-update) | async-done | bytes 8388624 | tf_op jit(solution)/shard_map/all_gather | solution.py:42
  66.4 3.9 gather_fusion
  70.3 3.4 fusion.72
  73.9 0.7 copy.157
  74.7 0.7 fusion.237
  75.4 2.8 collective-permute-start.3
  78.2 3.4 fusion.36
  81.6 3.6 fusion.16
  85.2 42.1 %all-gather.9.cloned.1.call-done = bf16[16,1024,256]{2,0,1:T(8,128)(2,1)} async-done(((bf16[16,32,256]{2,0,1:T(8,128)(2,1)}), bf16[16,1024,256]{2,0,1:T(8,128)(2,1)}) %all-gather.9.cloned.1.call-update) | async-done | bytes 8388624 | tf_op jit(solution)/shard_map/all_gather | solution.py:42
  127.3 3.9 gather_fusion.1
  131.2 3.4 fusion.6
  134.7 3.4 fusion.141
  138.2 0.7 copy.156
  139.0 0.7 fusion.236
  139.7 2.8 collective-permute-start.5
  142.5 3.4 fusion.34
  145.9 3.6 fusion.14
  149.6 42.1 %all-gather.11.cloned.1.call-done = bf16[16,1024,256]{2,0,1:T(8,128)(2,1)} async-done(((bf16[16,32,256]{2,0,1:T(8,128)(2,1)}), bf16[16,1024,256]{2,0,1:T(8,128)(2,1)}) %all-gather.11.cloned.1.call-update) | async-done | bytes 8388624 | tf_op jit(solution)/shard_map/all_gather | solution.py:42
  191.6 3.9 gather_fusion.2
  195.6 3.4 fusion.4
  199.0 3.4 fusion.129
  202.5 0.7 copy.155
  203.3 0.7 fusion.235
  204.0 2.8 collective-permute-start.7
  206.9 3.4 fusion.32
  210.3 3.6 fusion.12
  213.9 42.1 %all-gather.13.cloned.1.call-done = bf16[16,1024,256]{2,0,1:T(8,128)(2,1)} async-done(((bf16[16,32,256]{2,0,1:T(8,128)(2,1)}), bf16[16,1024,256]{2,0,1:T(8,128)(2,1)}) %all-gather.13.cloned.1.call-update) | async-done | bytes 8388624 | tf_op jit(solution)/shard_map/all_gather | solution.py:42
  256.0 3.9 gather_fusion.3
  259.9 3.4 fusion.2
  263.3 3.4 fusion.117
  266.8 0.9 fusion.230
  267.7 0.7 copy.154
  268.5 0.7 fusion.234
  269.2 2.8 collective-permute-start.9
  272.0 3.4 fusion.30
  275.5 3.8 fusion.10
  279.3 18.8 %all-gather.15.cloned.1.call-done = f32[64,8192]{1,0:T(8,128)} async-done(((f32[16,8192]{1,0:T(8,128)}), f32[64,8192]{1,0:T(8,128)}) %all-gather.15.cloned.1.call-update) | async-done | bytes 2097168 | tf_op jit(solution)/shard_map/all_gather | solution.py:55
  298.1 3.3 fusion.239
  301.5 51.9 %all-gather.17.cloned.1.call-done = bf16[16,1024,256]{2,0,1:T(8,128)(2,1)} async-done(((bf16[16,32,256]{2,0,1:T(8,128)(2,1)}), bf16[16,1024,256]{2,0,1:T(8,128)(2,1)}) %all-gather.17.cloned.1.call-update) | async-done | bytes 8388624 | tf_op jit(solution)/shard_map/all_gather | solution.py:42
  353.3 3.9 gather_fusion.4
  357.3 3.4 fusion
  360.7 3.6 fusion.105
  364.4 1.7 fusion.240
  366.1 126.6 %all-reduce = (f32[64,16]{0,1:T(8,128)S(1)}, f32[64,16]{0,1:T(8,128)S(1)}) all-reduce(f32[64,16]{0,1:T(8,128)S(1)} %fusion.239, f32[64,16]{0,1:T(8,128)S(1)} %fusion.240), channel_id=1, replica_groups=mesh['rows'=32,'cols'=4] {'rows'}, use_global_device_ids=true, to_apply=%region_0.2 | all-reduce | flops 2048 | bytes 16384 | tf_op jit(solution)/shard_map/psum | solution.py:59
  492.6 12.4 %all_gather.29 = f32[64,64]{0,1:T(8,128)S(1)} all-gather(f32[64,16]{0,1:T(8,128)S(1)} %get-tuple-element.3), channel_id=1, replica_groups=mesh['rows'=32,'cols'=4] {'cols'}, dimensions={1}, use_global_device_ids=true | all-gather | bytes 20480 | tf_op jit(solution)/shard_map/all_gather | solution.py:60
  505.1 0.1 copy.122
  505.2 5.8 %cholesky.17 = f32[64,64]{1,0:T(8,128)S(1)} custom-call(f32[64,64]{1,0:T(8,128)S(1)} %fusion.202), custom_call_target="Cholesky" | custom-call | tf_op jit(solution)/shard_map/jit(cholesky)/cholesky | solution.py:65
  511.1 0.6 compare_reduce_fusion
  511.7 0.7 fusion.199
  512.4 4.9 custom-call.6
  517.3 0.2 fusion.200
  517.5 11.9 %all_gather.31 = f32[64,64]{0,1:T(8,128)S(1)} all-gather(f32[64,16]{0,1:T(8,128)S(1)} %get-tuple-element.4), channel_id=1, replica_groups=mesh['rows'=32,'cols'=4] {'cols'}, dimensions={1}, use_global_device_ids=true | all-gather | bytes 20480 | tf_op jit(solution)/shard_map/all_gather | solution.py:64
  529.4 0.2 fusion.203
  529.6 0.2 fusion.241
  529.8 0.6 constant_dynamic-slice_fusion
  530.4 1.9 fusion.206
  (55 shorter events, 1.0 us)
Async XLA Ops:
  7.2 59.2 %all-gather.7.cloned.1.call-start = ((), (), s32[]{:S(2)}) async-start(), calls=%async_computation | async-start | bytes 8650752 | tf_op jit(solution)/shard_map/all_gather | solution.py:42
  9.0 118.3 %all-gather.9.cloned.1.call-start = ((), (), s32[]{:S(2)}) async-start(), calls=%async_computation.1 | async-start | bytes 8650752 | tf_op jit(solution)/shard_map/all_gather | solution.py:42
  9.8 10.1 %collective-permute-start = (bf16[16,1,256]{2,0,1:T(8,128)(2,1)S(1)}, bf16[16,1,256]{2,0,1:T(8,128)(2,1)S(1)}, u32[]{:S(2)}, u32[]{:S(2)}) collective-permute-start(bf16[16,1,256]{2,0,1:T(8,128)(2,1)S(1)} %get-tuple-element.24), channel_id=1, source_target_pairs={{0,4},{4,8},{8,12},{12,16},{16,20},{20,24},{24,28},{28,32},{32,36}... | collective-permute-start | bytes 24584 | tf_op jit(solution)/shard_map/ppermute | solution.py:15
  9.8 13.7 %collective-permute-start.1 = (bf16[16,1,256]{2,0,1:T(8,128)(2,1)S(1)}, bf16[16,1,256]{2,0,1:T(8,128)(2,1)S(1)}, u32[]{:S(2)}, u32[]{:S(2)}) collective-permute-start(bf16[16,1,256]{2,0,1:T(8,128)(2,1)S(1)} %get-tuple-element.23), channel_id=1, source_target_pairs={{4,0},{8,4},{12,8},{16,12},{20,16},{24,20},{28,24},{32,28},{36,32}... | collective-permute-start | bytes 24584 | tf_op jit(solution)/shard_map/ppermute | solution.py:18
  19.9 3.6 copy-start.4
  23.5 50.3 %copy-start.2 = (f32[16,8192]{1,0:T(8,128)S(1)}, f32[16,8192]{1,0:T(8,128)}, u32[]{:S(2)}) copy-start(f32[16,8192]{1,0:T(8,128)} %param.5) | copy-start | bytes 1572868
  74.6 117.0 %all-gather.11.cloned.1.call-start = ((), (), s32[]{:S(2)}) async-start(), calls=%async_computation.2 | async-start | bytes 8650752 | tf_op jit(solution)/shard_map/all_gather | solution.py:42
  75.4 6.2 %collective-permute-start.3 = (bf16[16,1,256]{2,0,1:T(8,128)(2,1)S(1)}, bf16[16,1,256]{2,0,1:T(8,128)(2,1)S(1)}, u32[]{:S(2)}, u32[]{:S(2)}) collective-permute-start(bf16[16,1,256]{2,0,1:T(8,128)(2,1)S(1)} %get-tuple-element.22), channel_id=1, source_target_pairs={{4,0},{8,4},{12,8},{16,12},{20,16},{24,20},{28,24},{32,28},{36,32}... | collective-permute-start | bytes 24584 | tf_op jit(solution)/shard_map/ppermute | solution.py:18
  81.6 53.1 %copy-start.5 = (bf16[2,32,8,256]{3,2,0,1:T(8,128)(2,1)S(1)}, bf16[2,32,8,256]{3,2,0,1:T(8,128)(2,1)}, u32[]{:S(2)}) copy-start(bf16[2,32,8,256]{3,2,0,1:T(8,128)(2,1)} %copy.157) | copy-start | bytes 786436
  81.6 53.1 %collective-permute-start.2 = (bf16[16,1,256]{2,0,1:T(8,128)(2,1)S(1)}, bf16[16,1,256]{2,0,1:T(8,128)(2,1)S(1)}, u32[]{:S(2)}, u32[]{:S(2)}) collective-permute-start(bf16[16,1,256]{2,0,1:T(8,128)(2,1)S(1)} %get-tuple-element.21), channel_id=1, source_target_pairs={{0,4},{4,8},{8,12},{12,16},{16,20},{20,24},{24,28},{28,32},{32,36}... | collective-permute-start | bytes 24584 | tf_op jit(solution)/shard_map/ppermute | solution.py:15
  138.9 117.0 %all-gather.13.cloned.1.call-start = ((), (), s32[]{:S(2)}) async-start(), calls=%async_computation.3 | async-start | bytes 8650752 | tf_op jit(solution)/shard_map/all_gather | solution.py:42
  139.7 6.2 %collective-permute-start.5 = (bf16[16,1,256]{2,0,1:T(8,128)(2,1)S(1)}, bf16[16,1,256]{2,0,1:T(8,128)(2,1)S(1)}, u32[]{:S(2)}, u32[]{:S(2)}) collective-permute-start(bf16[16,1,256]{2,0,1:T(8,128)(2,1)S(1)} %get-tuple-element.20), channel_id=1, source_target_pairs={{4,0},{8,4},{12,8},{16,12},{20,16},{24,20},{28,24},{32,28},{36,32}... | collective-permute-start | bytes 24584 | tf_op jit(solution)/shard_map/ppermute | solution.py:18
  145.9 53.1 %copy-start.6 = (bf16[2,32,8,256]{3,2,0,1:T(8,128)(2,1)S(1)}, bf16[2,32,8,256]{3,2,0,1:T(8,128)(2,1)}, u32[]{:S(2)}) copy-start(bf16[2,32,8,256]{3,2,0,1:T(8,128)(2,1)} %copy.156) | copy-start | bytes 786436
  145.9 53.1 %collective-permute-start.4 = (bf16[16,1,256]{2,0,1:T(8,128)(2,1)S(1)}, bf16[16,1,256]{2,0,1:T(8,128)(2,1)S(1)}, u32[]{:S(2)}, u32[]{:S(2)}) collective-permute-start(bf16[16,1,256]{2,0,1:T(8,128)(2,1)S(1)} %get-tuple-element.19), channel_id=1, source_target_pairs={{0,4},{4,8},{8,12},{12,16},{16,20},{20,24},{24,28},{28,32},{32,36}... | collective-permute-start | bytes 24584 | tf_op jit(solution)/shard_map/ppermute | solution.py:15
  203.3 94.9 %all-gather.15.cloned.1.call-start = ((), (), s32[]{:S(2)}) async-start(), calls=%async_computation.4 | async-start | bytes 2621440 | tf_op jit(solution)/shard_map/all_gather | solution.py:55
  204.0 6.2 %collective-permute-start.7 = (bf16[16,1,256]{2,0,1:T(8,128)(2,1)S(1)}, bf16[16,1,256]{2,0,1:T(8,128)(2,1)S(1)}, u32[]{:S(2)}, u32[]{:S(2)}) collective-permute-start(bf16[16,1,256]{2,0,1:T(8,128)(2,1)S(1)} %get-tuple-element.18), channel_id=1, source_target_pairs={{4,0},{8,4},{12,8},{16,12},{20,16},{24,20},{28,24},{32,28},{36,32}... | collective-permute-start | bytes 24584 | tf_op jit(solution)/shard_map/ppermute | solution.py:18
  210.3 53.1 %copy-start.7 = (bf16[2,32,8,256]{3,2,0,1:T(8,128)(2,1)S(1)}, bf16[2,32,8,256]{3,2,0,1:T(8,128)(2,1)}, u32[]{:S(2)}) copy-start(bf16[2,32,8,256]{3,2,0,1:T(8,128)(2,1)} %copy.155) | copy-start | bytes 786436
  210.3 53.1 %collective-permute-start.6 = (bf16[16,1,256]{2,0,1:T(8,128)(2,1)S(1)}, bf16[16,1,256]{2,0,1:T(8,128)(2,1)S(1)}, u32[]{:S(2)}, u32[]{:S(2)}) collective-permute-start(bf16[16,1,256]{2,0,1:T(8,128)(2,1)S(1)} %get-tuple-element.17), channel_id=1, source_target_pairs={{0,4},{4,8},{8,12},{12,16},{16,20},{20,24},{24,28},{28,32},{32,36}... | collective-permute-start | bytes 24584 | tf_op jit(solution)/shard_map/ppermute | solution.py:15
  267.7 85.7 %all-gather.17.cloned.1.call-start = ((), (), s32[]{:S(2)}) async-start(), calls=%async_computation.5 | async-start | bytes 8650752 | tf_op jit(solution)/shard_map/all_gather | solution.py:42
  269.2 6.2 %collective-permute-start.9 = (bf16[16,1,256]{2,0,1:T(8,128)(2,1)S(1)}, bf16[16,1,256]{2,0,1:T(8,128)(2,1)S(1)}, u32[]{:S(2)}, u32[]{:S(2)}) collective-permute-start(bf16[16,1,256]{2,0,1:T(8,128)(2,1)S(1)} %get-tuple-element.16), channel_id=1, source_target_pairs={{4,0},{8,4},{12,8},{16,12},{20,16},{24,20},{28,24},{32,28},{36,32}... | collective-permute-start | bytes 24584 | tf_op jit(solution)/shard_map/ppermute | solution.py:18
  275.4 22.7 %copy-start.1 = (f32[16,8192]{1,0:T(8,128)S(1)}, f32[16,8192]{1,0:T(8,128)}, u32[]{:S(2)}) copy-start(f32[16,8192]{1,0:T(8,128)} %get-tuple-element.6) | copy-start | bytes 1572868
  275.4 85.3 %copy-start.3 = (bf16[2,32,8,256]{3,2,0,1:T(8,128)(2,1)S(1)}, bf16[2,32,8,256]{3,2,0,1:T(8,128)(2,1)}, u32[]{:S(2)}) copy-start(bf16[2,32,8,256]{3,2,0,1:T(8,128)(2,1)} %copy.154) | copy-start | bytes 786436
  275.4 85.3 %collective-permute-start.8 = (bf16[16,1,256]{2,0,1:T(8,128)(2,1)S(1)}, bf16[16,1,256]{2,0,1:T(8,128)(2,1)S(1)}, u32[]{:S(2)}, u32[]{:S(2)}) collective-permute-start(bf16[16,1,256]{2,0,1:T(8,128)(2,1)S(1)} %get-tuple-element.15), channel_id=1, source_target_pairs={{0,4},{4,8},{8,12},{12,16},{16,20},{20,24},{24,28},{28,32},{32,36}... | collective-permute-start | bytes 24584 | tf_op jit(solution)/shard_map/ppermute | solution.py:15
  360.7 3.6 copy-start
Sparse Core Ops, SparseCore 0:
  10.8 55.4 all-gather.6
  74.7 52.5 all-gather.8
  139.1 52.5 all-gather.10
  203.4 52.5 all-gather.12
  267.8 30.2 all-gather.14
  300.2 53.0 all-gather.16
where the time goes:
time: 540 us; the launch traced here: 539 us
  waiting for transfers between devices  236 us (44%)
  blocking collectives  151 us (28%)
  matrix products  77.1 us (14%)
  local copies, waits for them, and re-layouts  27.9 us (5%)
  starting transfers between devices  17.6 us (3%)
  other arithmetic  14.9 us (3%)
  between operations  14.4 us (3%)
    all_gather x5, waiting for transfers between devices, apply_generator(): piece = lax.all_gather(shaped, 'rows', axis=1, tiled=True)  217 us
    psum x1, blocking collectives, body(): gram_mine = lax.psum(gram_part, 'rows')  127 us
    dot_general x20, matrix products, block_product(): jnp.einsum('jbt,bst->jbs', pieces, blocks[:, position], preferred_element...  69.5 us
    gather x5, local copies, waits for them, and re-layouts, apply_generator(): taken = jnp.take(piece, jnp.clip(far_cols, 0, piece.shape[1] - 1), axis=1)  19.7 us
    all_gather x1, waiting for transfers between devices, body(): whole_iterate = lax.all_gather(iterate, 'cols', axis=0, tiled=True)  18.8 us
    ppermute x5, starting transfers between devices, with_halo(): lax.ppermute(lax.slice_in_dim(block, 0, width, axis=dim), axis, backward)  17.3 us
    all_gather x1, blocking collectives, body(): gram = lax.all_gather(gram_mine, 'cols', axis=1, tiled=True) / total_states  12.4 us
    all_gather x1, blocking collectives, body(): lax.all_gather(product_mine, 'cols', axis=1, tiled=True) / total_states  11.9 us
  transfers between devices with their start and end apart: 16, of which 6 were waited for; matrix products, arithmetic and copies ran while one was open for 14% of the time, Pallas kernels for 0%

commit v1 on v0

--- a/solution.py
+++ b/solution.py
@@ -4,6 +4,16 @@
 from jax.sharding import PartitionSpec as P
 
 ITERS = 4
+
+
+def around_the_ring(shard, name, along):
+    n_dev = lax.axis_size(name)
+    held, blocks = (shard, [shard])
+    for _ in range(n_dev - 1):
+        held = lax.ppermute(held, name, [(i, (i + 1) % n_dev) for i in range(n_dev)])
+        blocks.insert(0, held)
+    merged = jnp.concatenate(blocks, axis=along)
+    return jnp.roll(merged, (lax.axis_index(name) + 1) * shard.shape[along], axis=along)
 
 
 def with_halo(block, sides, width):
@@ -52,7 +62,7 @@
     iterate = basis
     for step in range(ITERS):
         iterate = iterate + 0.2 * apply_generator(iterate.astype(jnp.bfloat16))
-    whole_iterate = lax.all_gather(iterate, "cols", axis=0, tiled=True)
+    whole_iterate = around_the_ring(iterate, "cols", 0)
     contract = (((1,), (1,)), ((), ()))
     gram_part = lax.dot_general(whole_iterate, iterate, contract, precision=highest)
     column_start = lax.axis_index("cols") * width

time: 540 us -> 509 us (0.943)
  waiting for transfers between devices: 236 us -> 203 us
    all_gather x5, waiting for transfers between devices: 217 us -> 171 us  [apply_generator(): piece = lax.all_gather(shaped, 'rows', axis=1, tiled=True)]
    ppermute x0 -> x3, waiting for transfers between devices: none -> 31.9 us  [around_the_ring(): lax.ppermute(held, name, [(i, (i + 1) % n_dev) for i in range(n_dev)])]
    all_gather x1 -> x0, waiting for transfers between devices: 18.8 us -> none  [body(): whole_iterate = lax.all_gather(iterate, 'cols', axis=0, tiled=True)]
  transfers between devices with their start and end apart: 16 -> 18, of which waited for: 6 -> 8; matrix products, arithmetic and copies ran while one was open for 14% -> 15% of each run, Pallas kernels for 0% -> 0%
where the time goes in v1:
time: 509 us; the launch traced here: 507 us
  waiting for transfers between devices  203 us (40%)
  blocking collectives  151 us (30%)
  matrix products  76.5 us (15%)
  local copies, waits for them, and re-layouts  30.1 us (6%)
  starting transfers between devices  18.3 us (4%)
  between operations  14.2 us (3%)
  other arithmetic  14.1 us (3%)
    all_gather x5, waiting for transfers between devices, apply_generator(): piece = lax.all_gather(shaped, 'rows', axis=1, tiled=True)  171 us
    psum x1, blocking collectives, body(): gram_mine = lax.psum(gram_part, 'rows')  127 us
    dot_general x20, matrix products, block_product(): jnp.einsum('jbt,bst->jbs', pieces, blocks[:, position], preferred_element...  68.9 us
    ppermute x3, waiting for transfers between devices, around_the_ring(): lax.ppermute(held, name, [(i, (i + 1) % n_dev) for i in range(n_dev)])  31.9 us
    gather x5, local copies, waits for them, and re-layouts, apply_generator(): taken = jnp.take(piece, jnp.clip(far_cols, 0, piece.shape[1] - 1), axis=1)  19.7 us
    ppermute x5, starting transfers between devices, with_halo(): lax.ppermute(lax.slice_in_dim(block, 0, width, axis=dim), axis, backward)  16.3 us
    all_gather x1, blocking collectives, body(): gram = lax.all_gather(gram_mine, 'cols', axis=1, tiled=True) / total_states  12.4 us
    all_gather x1, blocking collectives, body(): lax.all_gather(product_mine, 'cols', axis=1, tiled=True) / total_states  11.9 us
  transfers between devices with their start and end apart: 18, of which 8 were waited for; matrix products, arithmetic and copies ran while one was open for 15% of the time, Pallas kernels for 0%

profile of v1, /device:TPU:0, one launch (start us, length us, event | category | flops | bytes accessed | tf_op | source)
XLA Modules:
  0.0 507.3 jit_solution(8983625059101979984)
XLA Ops:
  7.2 1.1 convert_element_type.16
  8.3 0.7 copy.158
  9.1 0.7 fusion.245
  9.8 6.0 %collective-permute-start.1 = (bf16[16,1,256]{2,0,1:T(8,128)(2,1)S(1)}, bf16[16,1,256]{2,0,1:T(8,128)(2,1)S(1)}, u32[]{:S(2)}, u32[]{:S(2)}) collective-permute-start(bf16[16,1,256]{2,0,1:T(8,128)(2,1)S(1)} %get-tuple-element.23), channel_id=1, source_target_pairs={{4,0},{8,4},{12,8},{16,12},{20,16},{24,20},{28,24},{32,28},{36,32}... | collective-permute-start | bytes 24584 | tf_op jit(solution)/shard_map/ppermute | solution.py:28
  15.8 0.7 compare_and_fusion
  16.5 3.4 fusion.66
  19.9 3.4 fusion.90
  23.3 3.5 fusion.87
  26.8 39.6 %all-gather.6.cloned.1.call-done = bf16[16,1024,256]{2,0,1:T(8,128)(2,1)} async-done(((bf16[16,32,256]{2,0,1:T(8,128)(2,1)}), bf16[16,1024,256]{2,0,1:T(8,128)(2,1)}) %all-gather.6.cloned.1.call-update) | async-done | bytes 8388624 | tf_op jit(solution)/shard_map/all_gather | solution.py:52
  66.4 3.9 gather_fusion
  70.3 3.4 fusion.78
  73.9 0.7 copy.157
  74.7 0.7 fusion.244
  75.4 2.8 collective-permute-start.3
  78.2 3.4 fusion.36
  81.6 3.4 fusion.16
  85.0 42.2 %all-gather.8.cloned.1.call-done = bf16[16,1024,256]{2,0,1:T(8,128)(2,1)} async-done(((bf16[16,32,256]{2,0,1:T(8,128)(2,1)}), bf16[16,1024,256]{2,0,1:T(8,128)(2,1)}) %all-gather.8.cloned.1.call-update) | async-done | bytes 8388624 | tf_op jit(solution)/shard_map/all_gather | solution.py:52
  127.3 3.9 gather_fusion.1
  131.2 3.4 fusion.6
  134.6 3.4 fusion.147
  138.2 0.7 copy.156
  139.0 0.7 fusion.243
  139.7 2.8 collective-permute-start.5
  142.5 3.4 fusion.34
  145.9 3.4 fusion.14
  149.4 42.2 %all-gather.10.cloned.1.call-done = bf16[16,1024,256]{2,0,1:T(8,128)(2,1)} async-done(((bf16[16,32,256]{2,0,1:T(8,128)(2,1)}), bf16[16,1024,256]{2,0,1:T(8,128)(2,1)}) %all-gather.10.cloned.1.call-update) | async-done | bytes 8388624 | tf_op jit(solution)/shard_map/all_gather | solution.py:52
  191.6 3.9 gather_fusion.2
  195.6 3.4 fusion.4
  199.0 3.4 fusion.135
  202.5 0.7 copy.155
  203.3 0.7 fusion.242
  204.0 2.8 collective-permute-start.7
  206.8 3.4 fusion.32
  210.2 3.4 fusion.12
  213.7 42.2 %all-gather.12.cloned.1.call-done = bf16[16,1024,256]{2,0,1:T(8,128)(2,1)} async-done(((bf16[16,32,256]{2,0,1:T(8,128)(2,1)}), bf16[16,1024,256]{2,0,1:T(8,128)(2,1)}) %all-gather.12.cloned.1.call-update) | async-done | bytes 8388624 | tf_op jit(solution)/shard_map/all_gather | solution.py:52
  255.9 3.9 gather_fusion.3
  259.9 3.4 fusion.2
  263.3 3.4 fusion.123
  266.8 0.7 copy.154
  267.6 1.5 collective-permute-start.8
  269.1 13.8 %collective-permute-done.8 = f32[16,8192]{1,0:T(8,128)S(1)} collective-permute-done((f32[16,8192]{1,0:T(8,128)S(1)}, f32[16,8192]{1,0:T(8,128)S(1)}, u32[]{:S(2)}, u32[]{:S(2)}) %collective-permute-start.8) | collective-permute-done | bytes 524320 | tf_op jit(solution)/shard_map/ppermute | solution.py:13
  282.9 0.3 collective-permute-start.9
  283.2 0.7 fusion.241
  283.9 1.8 collective-permute-start.12
  285.8 3.4 fusion.30
  289.2 8.4 %collective-permute-done.9 = f32[16,8192]{1,0:T(8,128)S(1)} collective-permute-done((f32[16,8192]{1,0:T(8,128)S(1)}, f32[16,8192]{1,0:T(8,128)S(1)}, u32[]{:S(2)}, u32[]{:S(2)}) %collective-permute-start.9) | collective-permute-done | bytes 524320 | tf_op jit(solution)/shard_map/ppermute | solution.py:13
  297.6 4.0 fusion.10
  301.5 9.7 %collective-permute-done.10 = f32[16,8192]{1,0:T(8,128)S(1)} collective-permute-done((f32[16,8192]{1,0:T(8,128)S(1)}, f32[16,8192]{1,0:T(8,128)S(1)}, u32[]{:S(2)}, u32[]{:S(2)}) %collective-permute-start.10) | collective-permute-done | bytes 524320 | tf_op jit(solution)/shard_map/ppermute | solution.py:13
  311.6 2.0 copy-done
  313.6 1.7 fusion.64
  315.3 5.0 all-gather.14.cloned.1.call-done
  320.3 3.9 gather_fusion.4
  324.2 3.4 fusion
  327.6 3.5 fusion.111
  331.2 1.8 fusion.60
  333.0 126.6 %all-reduce = (f32[64,16]{0,1:T(8,128)S(1)}, f32[64,16]{0,1:T(8,128)S(1)}) all-reduce(f32[64,16]{0,1:T(8,128)S(1)} %fusion.64, f32[64,16]{0,1:T(8,128)S(1)} %fusion.60), channel_id=1, replica_groups=mesh['rows'=32,'cols'=4] {'rows'}, use_global_device_ids=true, to_apply=%region_0.2 | all-reduce | flops 2048 | bytes 16384 | tf_op jit(solution)/shard_map/psum | solution.py:69
  459.6 12.4 %all_gather.25 = f32[64,64]{0,1:T(8,128)S(1)} all-gather(f32[64,16]{0,1:T(8,128)S(1)} %get-tuple-element.3), channel_id=1, replica_groups=mesh['rows'=32,'cols'=4] {'cols'}, dimensions={1}, use_global_device_ids=true | all-gather | bytes 20480 | tf_op jit(solution)/shard_map/all_gather | solution.py:70
  472.1 5.8 %cholesky.17 = f32[64,64]{1,0:T(8,128)S(1)} custom-call(f32[64,64]{1,0:T(8,128)S(1)} %fusion.208), custom_call_target="Cholesky" | custom-call | tf_op jit(solution)/shard_map/jit(cholesky)/cholesky | solution.py:75
  478.0 0.6 compare_reduce_fusion
  478.6 0.7 fusion.205
  479.3 4.9 custom-call.6
  484.4 11.9 %all_gather.27 = f32[64,64]{0,1:T(8,128)S(1)} all-gather(f32[64,16]{0,1:T(8,128)S(1)} %get-tuple-element.4), channel_id=1, replica_groups=mesh['rows'=32,'cols'=4] {'cols'}, dimensions={1}, use_global_device_ids=true | all-gather | bytes 20480 | tf_op jit(solution)/shard_map/all_gather | solution.py:74
  496.7 3.5 fusion.62
  500.2 0.6 constant_dynamic-slice_fusion
  (66 shorter events, 1.8 us)
Async XLA Ops:
  7.2 59.2 %all-gather.6.cloned.1.call-start = ((), (), s32[]{:S(2)}) async-start(), calls=%async_computation | async-start | bytes 8650752 | tf_op jit(solution)/shard_map/all_gather | solution.py:52
  9.0 10.9 %copy-start.4 = (bf16[2,32,8,256]{3,2,0,1:T(8,128)(2,1)S(1)}, bf16[2,32,8,256]{3,2,0,1:T(8,128)(2,1)}, u32[]{:S(2)}) copy-start(bf16[2,32,8,256]{3,2,0,1:T(8,128)(2,1)} %copy.158) | copy-start | bytes 786436
  9.0 118.3 %all-gather.8.cloned.1.call-start = ((), (), s32[]{:S(2)}) async-start(), calls=%async_computation.1 | async-start | bytes 8650752 | tf_op jit(solution)/shard_map/all_gather | solution.py:52
  9.8 10.1 %collective-permute-start = (bf16[16,1,256]{2,0,1:T(8,128)(2,1)S(1)}, bf16[16,1,256]{2,0,1:T(8,128)(2,1)S(1)}, u32[]{:S(2)}, u32[]{:S(2)}) collective-permute-start(bf16[16,1,256]{2,0,1:T(8,128)(2,1)S(1)} %get-tuple-element.24), channel_id=1, source_target_pairs={{0,4},{4,8},{8,12},{12,16},{16,20},{20,24},{24,28},{28,32},{32,36}... | collective-permute-start | bytes 24584 | tf_op jit(solution)/shard_map/ppermute | solution.py:25
  9.8 13.5 %collective-permute-start.1 = (bf16[16,1,256]{2,0,1:T(8,128)(2,1)S(1)}, bf16[16,1,256]{2,0,1:T(8,128)(2,1)S(1)}, u32[]{:S(2)}, u32[]{:S(2)}) collective-permute-start(bf16[16,1,256]{2,0,1:T(8,128)(2,1)S(1)} %get-tuple-element.23), channel_id=1, source_target_pairs={{4,0},{8,4},{12,8},{16,12},{20,16},{24,20},{28,24},{32,28},{36,32}... | collective-permute-start | bytes 24584 | tf_op jit(solution)/shard_map/ppermute | solution.py:28
  26.8 47.0 %copy-start.2 = (f32[16,8192]{1,0:T(8,128)S(1)}, f32[16,8192]{1,0:T(8,128)}, u32[]{:S(2)}) copy-start(f32[16,8192]{1,0:T(8,128)} %param.5) | copy-start | bytes 1572868
  74.6 7.0 %copy-start.5 = (bf16[2,32,8,256]{3,2,0,1:T(8,128)(2,1)S(1)}, bf16[2,32,8,256]{3,2,0,1:T(8,128)(2,1)}, u32[]{:S(2)}) copy-start(bf16[2,32,8,256]{3,2,0,1:T(8,128)(2,1)} %copy.157) | copy-start | bytes 786436
  74.6 117.0 %all-gather.10.cloned.1.call-start = ((), (), s32[]{:S(2)}) async-start(), calls=%async_computation.2 | async-start | bytes 8650752 | tf_op jit(solution)/shard_map/all_gather | solution.py:52
  75.4 6.2 %collective-permute-start.3 = (bf16[16,1,256]{2,0,1:T(8,128)(2,1)S(1)}, bf16[16,1,256]{2,0,1:T(8,128)(2,1)S(1)}, u32[]{:S(2)}, u32[]{:S(2)}) collective-permute-start(bf16[16,1,256]{2,0,1:T(8,128)(2,1)S(1)} %get-tuple-element.22), channel_id=1, source_target_pairs={{4,0},{8,4},{12,8},{16,12},{20,16},{24,20},{28,24},{32,28},{36,32}... | collective-permute-start | bytes 24584 | tf_op jit(solution)/shard_map/ppermute | solution.py:28
  81.6 53.1 %collective-permute-start.2 = (bf16[16,1,256]{2,0,1:T(8,128)(2,1)S(1)}, bf16[16,1,256]{2,0,1:T(8,128)(2,1)S(1)}, u32[]{:S(2)}, u32[]{:S(2)}) collective-permute-start(bf16[16,1,256]{2,0,1:T(8,128)(2,1)S(1)} %get-tuple-element.21), channel_id=1, source_target_pairs={{0,4},{4,8},{8,12},{12,16},{16,20},{20,24},{24,28},{28,32},{32,36}... | collective-permute-start | bytes 24584 | tf_op jit(solution)/shard_map/ppermute | solution.py:25
  138.9 7.0 %copy-start.6 = (bf16[2,32,8,256]{3,2,0,1:T(8,128)(2,1)S(1)}, bf16[2,32,8,256]{3,2,0,1:T(8,128)(2,1)}, u32[]{:S(2)}) copy-start(bf16[2,32,8,256]{3,2,0,1:T(8,128)(2,1)} %copy.156) | copy-start | bytes 786436
  138.9 117.0 %all-gather.12.cloned.1.call-start = ((), (), s32[]{:S(2)}) async-start(), calls=%async_computation.3 | async-start | bytes 8650752 | tf_op jit(solution)/shard_map/all_gather | solution.py:52
  139.7 6.2 %collective-permute-start.5 = (bf16[16,1,256]{2,0,1:T(8,128)(2,1)S(1)}, bf16[16,1,256]{2,0,1:T(8,128)(2,1)S(1)}, u32[]{:S(2)}, u32[]{:S(2)}) collective-permute-start(bf16[16,1,256]{2,0,1:T(8,128)(2,1)S(1)} %get-tuple-element.20), channel_id=1, source_target_pairs={{4,0},{8,4},{12,8},{16,12},{20,16},{24,20},{28,24},{32,28},{36,32}... | collective-permute-start | bytes 24584 | tf_op jit(solution)/shard_map/ppermute | solution.py:28
  145.9 53.1 %collective-permute-start.4 = (bf16[16,1,256]{2,0,1:T(8,128)(2,1)S(1)}, bf16[16,1,256]{2,0,1:T(8,128)(2,1)S(1)}, u32[]{:S(2)}, u32[]{:S(2)}) collective-permute-start(bf16[16,1,256]{2,0,1:T(8,128)(2,1)S(1)} %get-tuple-element.19), channel_id=1, source_target_pairs={{0,4},{4,8},{8,12},{12,16},{16,20},{20,24},{24,28},{28,32},{32,36}... | collective-permute-start | bytes 24584 | tf_op jit(solution)/shard_map/ppermute | solution.py:25
  203.2 7.0 %copy-start.7 = (bf16[2,32,8,256]{3,2,0,1:T(8,128)(2,1)S(1)}, bf16[2,32,8,256]{3,2,0,1:T(8,128)(2,1)}, u32[]{:S(2)}) copy-start(bf16[2,32,8,256]{3,2,0,1:T(8,128)(2,1)} %copy.155) | copy-start | bytes 786436
  203.3 117.0 %all-gather.14.cloned.1.call-start = ((), (), s32[]{:S(2)}) async-start(), calls=%async_computation.4 | async-start | bytes 8650752 | tf_op jit(solution)/shard_map/all_gather | solution.py:52
  204.0 6.2 %collective-permute-start.7 = (bf16[16,1,256]{2,0,1:T(8,128)(2,1)S(1)}, bf16[16,1,256]{2,0,1:T(8,128)(2,1)S(1)}, u32[]{:S(2)}, u32[]{:S(2)}) collective-permute-start(bf16[16,1,256]{2,0,1:T(8,128)(2,1)S(1)} %get-tuple-element.18), channel_id=1, source_target_pairs={{4,0},{8,4},{12,8},{16,12},{20,16},{24,20},{28,24},{32,28},{36,32}... | collective-permute-start | bytes 24584 | tf_op jit(solution)/shard_map/ppermute | solution.py:28
  210.2 53.1 %collective-permute-start.6 = (bf16[16,1,256]{2,0,1:T(8,128)(2,1)S(1)}, bf16[16,1,256]{2,0,1:T(8,128)(2,1)S(1)}, u32[]{:S(2)}, u32[]{:S(2)}) collective-permute-start(bf16[16,1,256]{2,0,1:T(8,128)(2,1)S(1)} %get-tuple-element.17), channel_id=1, source_target_pairs={{0,4},{4,8},{8,12},{12,16},{16,20},{20,24},{24,28},{28,32},{32,36}... | collective-permute-start | bytes 24584 | tf_op jit(solution)/shard_map/ppermute | solution.py:25
  267.5 30.0 %copy-start.3 = (bf16[2,32,8,256]{3,2,0,1:T(8,128)(2,1)S(1)}, bf16[2,32,8,256]{3,2,0,1:T(8,128)(2,1)}, u32[]{:S(2)}) copy-start(bf16[2,32,8,256]{3,2,0,1:T(8,128)(2,1)} %copy.154) | copy-start | bytes 786436
  267.6 15.4 %collective-permute-start.8 = (f32[16,8192]{1,0:T(8,128)S(1)}, f32[16,8192]{1,0:T(8,128)S(1)}, u32[]{:S(2)}, u32[]{:S(2)}) collective-permute-start(f32[16,8192]{1,0:T(8,128)S(1)} %get-tuple-element.6), channel_id=1, source_target_pairs={{0,1},{1,2},{2,3},{3,0},{4,5},{5,6},{6,7},{7,4},{8,9},{9,10},{10,1... | collective-permute-start | bytes 1572872 | tf_op jit(solution)/shard_map/ppermute | solution.py:13
  282.9 14.6 %collective-permute-start.9 = (f32[16,8192]{1,0:T(8,128)S(1)}, f32[16,8192]{1,0:T(8,128)S(1)}, u32[]{:S(2)}, u32[]{:S(2)}) collective-permute-start(f32[16,8192]{1,0:T(8,128)S(1)} %collective-permute-done.8), channel_id=1, source_target_pairs={{0,1},{1,2},{2,3},{3,0},{4,5},{5,6},{6,7},{7,4},{8,9},{9,10},{10,1... | collective-permute-start | bytes 1572872 | tf_op jit(solution)/shard_map/ppermute | solution.py:13
  283.9 13.6 %collective-permute-start.12 = (bf16[16,1,256]{2,0,1:T(8,128)(2,1)S(1)}, bf16[16,1,256]{2,0,1:T(8,128)(2,1)S(1)}, u32[]{:S(2)}, u32[]{:S(2)}) collective-permute-start(bf16[16,1,256]{2,0,1:T(8,128)(2,1)S(1)} %get-tuple-element.16), channel_id=1, source_target_pairs={{4,0},{8,4},{12,8},{16,12},{20,16},{24,20},{28,24},{32,28},{36,32}... | collective-permute-start | bytes 24584 | tf_op jit(solution)/shard_map/ppermute | solution.py:28
  289.2 38.5 %collective-permute-start.11 = (bf16[16,1,256]{2,0,1:T(8,128)(2,1)S(1)}, bf16[16,1,256]{2,0,1:T(8,128)(2,1)S(1)}, u32[]{:S(2)}, u32[]{:S(2)}) collective-permute-start(bf16[16,1,256]{2,0,1:T(8,128)(2,1)S(1)} %get-tuple-element.15), channel_id=1, source_target_pairs={{0,4},{4,8},{8,12},{12,16},{16,20},{20,24},{24,28},{28,32},{32,36}... | collective-permute-start | bytes 24584 | tf_op jit(solution)/shard_map/ppermute | solution.py:25
  297.5 13.7 %collective-permute-start.10 = (f32[16,8192]{1,0:T(8,128)S(1)}, f32[16,8192]{1,0:T(8,128)S(1)}, u32[]{:S(2)}, u32[]{:S(2)}) collective-permute-start(f32[16,8192]{1,0:T(8,128)S(1)} %collective-permute-done.9), channel_id=1, source_target_pairs={{0,1},{1,2},{2,3},{3,0},{4,5},{5,6},{6,7},{7,4},{8,9},{9,10},{10,1... | collective-permute-start | bytes 1572872 | tf_op jit(solution)/shard_map/ppermute | solution.py:13
  311.6 2.0 copy-start
  327.6 3.6 copy-start.1
Sparse Core Ops, SparseCore 0:
  10.8 55.4 all-gather.5
  74.7 52.5 all-gather.7
  139.0 52.5 all-gather.9
  203.4 52.5 all-gather.11
  267.7 52.5 all-gather.13
